TPU v7x, 32 devices: a whole 2x2x4 slice. The times are simulated.
32 devices in a mesh: grp: 2 (over x), row: 8 (over z, y), col: 2 (over core).
Axes of the slice: x: 2, y: 2, z: 4, core: 2. Of those that a mesh axis runs over, the one named last changes fastest.
Arguments:
- alignment_left: bfloat16 [128, 32, 256], P('col', None, ('grp', 'row')), parts along dimension 2, may hold values from -10 to 10
- alignment_right: bfloat16 [128, 32, 256], P('col', None, ('grp', 'row')), parts along dimension 2, may hold values from -10 to 10
- weight: bfloat16 [1024, 128], replicated, may hold values from -0.1875 to 0.1875
- pairwise_bias: bfloat16 [128], replicated, may hold values from -3 to 3
- cotangent: bfloat16 [256, 128, 128], P(('grp', 'row'), 'col'), parts along dimension 0, may hold values from -6 to 6
Outputs:
- pair_update: bfloat16 [256, 128, 128], P(('grp', 'row'), 'col'), parts along dimension 0
- grad_left: float32 [128, 32, 256], P('col', None, ('grp', 'row')), parts along dimension 2
- grad_right: float32 [128, 32, 256], P('col', None, ('grp', 'row')), parts along dimension 2
- grad_weight: float32 [2048, 128], P('grp'), parts along dimension 0
- grad_bias: float32 [256], P('grp'), parts along dimension 0
There are 2 independent parts, one for each index of `grp`. A program takes and returns all parts, laid end to end along the dimension named above; an argument that names none is the same for every part. Nothing has to cross between parts.
All inputs are finite; a program needn't handle non-finite values.
Results may differ from a plain program's by a relative error of at most 0.0034.
Values may be sent and summed in bfloat16 or wider, within the bound.
A program may use at most 128 MiB of HBM per device.

v0:
```python
import math

import jax
import jax.numpy as jnp
from jax import lax
from jax.sharding import PartitionSpec as P


def pair_block(
    row_side, col_side, weight, pairwise_bias, cotangent, col_start, block_cols, state_tuple
):
    pair_out, weight_acc, rows_acc, cols_acc = state_tuple
    sequence_total, channel_count, row_count = row_side.shape
    inv_seqs = 1.0 / sequence_total
    cols_part = lax.dynamic_slice_in_dim(col_side, col_start, block_cols, 2)
    grad_part = lax.dynamic_slice_in_dim(cotangent, col_start, block_cols, 1)
    outer_tile = jnp.einsum(
        "sci,sdj->ijcd", row_side, cols_part, preferred_element_type=jnp.float32
    )
    outer_tile = (
        (outer_tile * inv_seqs)
        .astype(jnp.bfloat16)
        .reshape(row_count * block_cols, channel_count * channel_count)
    )
    projected = jnp.dot(
        outer_tile, weight, preferred_element_type=jnp.float32
    ) + pairwise_bias.astype(jnp.float32)
    projected = projected.astype(jnp.bfloat16).reshape(row_count, block_cols, weight.shape[1])
    pair_out = lax.dynamic_update_slice_in_dim(pair_out, projected, col_start, 1)
    flat_grad = grad_part.reshape(row_count * block_cols, weight.shape[1])
    grad_outer = jnp.dot(flat_grad, weight.T, preferred_element_type=jnp.float32)
    grad_outer = grad_outer.astype(jnp.bfloat16).reshape(
        row_count, block_cols, channel_count, channel_count
    )
    weight_acc = weight_acc + lax.dot_general(
        outer_tile, flat_grad, (((0,), (0,)), ((), ())), preferred_element_type=jnp.float32
    )
    rows_acc = (
        rows_acc
        + jnp.einsum("ijcd,sdj->sci", grad_outer, cols_part, preferred_element_type=jnp.float32)
        * inv_seqs
    )
    cols_term = (
        jnp.einsum("ijcd,sci->sdj", grad_outer, row_side, preferred_element_type=jnp.float32)
        * inv_seqs
    )
    cols_acc = lax.dynamic_update_slice_in_dim(cols_acc, cols_term, col_start, 2)
    return (pair_out, weight_acc, rows_acc, cols_acc)


def local(alignment_left, alignment_right, weight, pairwise_bias, cotangent):
    row_count = cotangent.shape[0]
    col_total = cotangent.shape[1]
    row_side = lax.all_gather(alignment_left, "col", axis=0, tiled=True)
    gathered = lax.all_gather(alignment_right, "row", axis=2, tiled=True)
    col_side = lax.all_to_all(gathered, "col", split_axis=2, concat_axis=0, tiled=True)
    sequence_total, channel_count = (row_side.shape[0], row_side.shape[1])
    block_cols = math.gcd(64, col_total)
    initial = (
        jnp.zeros(cotangent.shape, jnp.bfloat16),
        jnp.zeros((channel_count * channel_count, weight.shape[1]), jnp.float32),
        jnp.zeros(row_side.shape, jnp.float32),
        jnp.zeros(col_side.shape, jnp.float32),
    )

    def step_fn(block_index, state_tuple):
        return pair_block(
            row_side,
            col_side,
            weight,
            pairwise_bias,
            cotangent,
            block_index * block_cols,
            block_cols,
            state_tuple,
        )

    pair_out, weight_acc, rows_acc, cols_acc = lax.fori_loop(
        0, col_total // block_cols, step_fn, initial
    )
    bias_term = jnp.sum(cotangent.astype(jnp.float32), axis=(0, 1))
    grad_left = lax.psum_scatter(rows_acc, "col", scatter_dimension=0, tiled=True)
    returned = lax.all_to_all(cols_acc, "col", split_axis=0, concat_axis=2, tiled=True)
    grad_right = lax.psum_scatter(returned, "row", scatter_dimension=2, tiled=True)
    weight_sum, bias_sum = lax.psum((weight_acc, bias_term), ("row", "col"))
    inv_rows = 1.0 / (row_count * lax.axis_size("row"))
    return (pair_out, grad_left, grad_right, weight_sum * inv_rows, bias_sum * inv_rows)


def solution(mesh):
    in_specs = (
        P("col", None, ("grp", "row")),
        P("col", None, ("grp", "row")),
        P(),
        P(),
        P(("grp", "row"), "col", None),
    )
    out_specs = (
        P(("grp", "row"), "col", None),
        P("col", None, ("grp", "row")),
        P("col", None, ("grp", "row")),
        P("grp", None),
        P("grp"),
    )
    return jax.shard_map(local, mesh=mesh, in_specs=in_specs, out_specs=out_specs, check_vma=False)
```

profile of v0, /device:TPU:0, one launch (start us, length us, event | category | flops | bytes accessed | tf_op | source)
XLA Modules:
  0.0 191.1 jit_solution(6953676016295786206)
XLA Ops:
  8.0 0.0 copy-start
  8.0 1.0 copy.35
  9.0 34.6 %all_gather.6 = bf16[64,32,128]{0,1,2:T(8,128)(2,1)S(1)} all-gather(bf16[64,32,16]{0,1,2:T(8,128)(2,1)S(1)} %copy.35), channel_id=1, replica_groups=mesh['grp'=2,'row'=8,'col'=2] {'row'}, dimensions={2}, use_global_device_ids=true | all-gather | bytes 589824 | tf_op jit(solution)/shard_map/all_gather | solution.py:55
  43.6 1.5 reshape.39
  45.1 3.5 %all-to-all-start = ((bf16[2,2,65536]{2,1,0:T(2,128)(2,1)}), bf16[2,2,65536]{2,1,0:T(2,128)(2,1)S(1)}, u32[]{:S(2)}, u32[]{:S(2)}) async-start(bf16[2,2,65536]{2,1,0:T(2,128)(2,1)} %reshape.39), calls=%async_computation | async-start | bytes 1048576 | tf_op jit(solution)/shard_map/all_to_all | solution.py:56
  48.6 0.0 all-reduce.2.cloned.1.call-start
  48.6 1.2 copy.37
  49.9 2.3 %all_gather.7 = bf16[128,32,16]{1,2,0:T(8,128)(2,1)S(1)} all-gather(bf16[64,32,16]{1,2,0:T(8,128)(2,1)S(1)} %copy.37), channel_id=1, replica_groups=mesh['grp'=2,'row'=8,'col'=2] {'col'}, dimensions={0}, use_global_device_ids=true | all-gather | bytes 196608 | tf_op jit(solution)/shard_map/all_gather | solution.py:54
  52.1 0.4 copy.38
  52.5 0.0 all-to-all-done
  52.6 0.7 reshape.40
  53.3 1.1 copy.56
  54.4 0.5 reshape.31
  54.9 0.0 copy-start.3
  54.9 1.3 fusion
  56.2 0.0 copy-done.3
  56.2 3.5 %copy.39 = bf16[16,64,32,32]{1,0,3,2:T(8,128)(2,1)} copy(bf16[16,64,32,32]{1,2,0,3:T(8,128)(2,1)S(1)} %fusion) | data formatting | bytes 4194304 | tf_op jit(solution)/shard_map/while/body/eval_jaxpr/convert_element_type | solution.py:22
  59.7 0.0 copy-start.1
  59.7 5.5 %reshape.27 = bf16[1024,1024]{0,1:T(8,128)(2,1)S(1)} reshape(bf16[16,64,32,32]{1,0,3,2:T(8,128)(2,1)} %copy.39) | data formatting | bytes 4194304 | tf_op jit(solution)/shard_map/while/body/eval_jaxpr/reshape | solution.py:23
  65.2 0.0 copy-done.1
  65.2 1.5 fusion.8
  66.8 0.0 all-reduce.2.cloned.1.call-update
  66.8 0.0 reduce-scatter.7.cloned.1.call-start
  66.9 0.0 copy-done
  66.9 2.1 %convolution_convert_fusion = bf16[1024,1024]{1,0:T(8,128)(2,1)} fusion(bf16[1024,128]{1,0:T(8,128)(2,1)S(1)} %bitcast.67, bf16[1024,128]{1,0:T(8,128)(2,1)S(1)} %copy-done), kind=kOutput, calls=%fused_computation.2 | convolution fusion | flops 269484032 | bytes 2621440 | tf_op jit(solution)/shard_map/while/body/eval_jaxpr/dot_general | solution.py:31
  68.9 0.0 copy-start.4
  68.9 4.0 %copy.40 = bf16[1024,1024]{0,1:T(8,128)(2,1)} copy(bf16[1024,1024]{1,0:T(8,128)(2,1)} %convolution_convert_fusion) | data formatting | bytes 4194304 | tf_op jit(solution)/shard_map/while/body/eval_jaxpr/convert_element_type | solution.py:32
  72.9 6.4 %reshape.30 = bf16[16,64,32,32]{1,0,3,2:T(8,128)(2,1)} reshape(bf16[1024,1024]{0,1:T(8,128)(2,1)} %copy.40) | data formatting | bytes 4194304 | tf_op jit(solution)/shard_map/while/body/eval_jaxpr/reshape | solution.py:32
  79.3 0.0 copy-done.4
  79.3 3.8 %fusion.5 = f32[128,32,16]{0,2,1:T(8,128)} fusion(bf16[16,64,32,32]{1,0,3,2:T(8,128)(2,1)} %reshape.30, bf16[128,32,64,1]{0,2,1,3:T(8,128)(2,1)S(1)} %copy-done.4), kind=kOutput, calls=%fused_computation.10 | convolution fusion | flops 268500992 | bytes 2883584 | tf_op jit(solution)/shard_map/while/body/eval_jaxpr/ijcd,sdj->sci/dot_general | solution.py:40
  83.1 2.4 %copy.51 = f32[128,32,16]{1,2,0:T(8,128)} copy(f32[128,32,16]{0,2,1:T(8,128)} %fusion.5) | data formatting | bytes 524288
  85.5 2.3 %reshape.37 = f32[128,512]{1,0:T(8,128)} reshape(f32[128,16,32]{2,1,0:T(8,128)} %bitcast.62) | data formatting | bytes 524288
  87.8 0.0 reduce-scatter.7.cloned.1.call-update
  87.8 0.2 reduce-scatter.5.cloned.1.call-start
  88.1 0.5 copy.48
  88.6 3.5 %fusion.2 = f32[128,32,64]{0,2,1:T(8,128)S(1)} fusion(bf16[16,64,32,32]{1,0,3,2:T(8,128)(2,1)} %reshape.30, bf16[128,32,16,1]{0,2,3,1:T(8,128)(2,1)S(1)} %copy.48), kind=kOutput, calls=%fused_computation.5 | convolution fusion | flops 268697600 | bytes 3276800 | tf_op jit(solution)/shard_map/while/body/eval_jaxpr/ijcd,sci->sdj/dot_general | solution.py:44
  92.1 2.8 %copy.43 = f32[128,32,64]{2,1,0:T(8,128)} copy(f32[128,32,64]{0,2,1:T(8,128)S(1)} %fusion.2) | data formatting | bytes 2097152 | tf_op jit(solution)/shard_map/while/body/eval_jaxpr/mul | solution.py:44
  94.9 2.6 %reshape.41 = f32[2,1,131072]{2,1,0:T(1,128)S(1)} reshape(f32[128,32,64]{2,1,0:T(8,128)} %copy.43) | data formatting | bytes 2097152
  97.5 5.4 %all_to_all.36 = f32[2,1,131072]{2,1,0:T(1,128)} all-to-all(f32[2,1,131072]{2,1,0:T(1,128)S(1)} %reshape.41), channel_id=1, replica_groups=mesh['grp'=2,'row'=8,'col'=2] {'col'}, dimensions={0} | all-to-all | bytes 2097152 | tf_op jit(solution)/shard_map/all_to_all | solution.py:83
  102.8 0.5 broadcast.25
  103.4 4.9 %reduce = f32[2,131072]{1,0:T(2,128)S(1)} reduce(f32[2,1,131072]{2,1,0:T(1,128)} %all_to_all.36, f32[]{:T(128)} %broadcast.25), dimensions={1}, to_apply=%all_to_all.30.reduce_sub_computation | reduce | bytes 2097156 | tf_op jit(solution)/shard_map/all_to_all | solution.py:83
  108.3 0.0 copy-start.5
  108.3 2.5 %reshape.42 = f32[128,32,64]{2,1,0:T(8,128)} reshape(f32[2,131072]{1,0:T(2,128)S(1)} %reduce) | data formatting | bytes 2097152
  110.8 0.0 copy-start.2
  110.8 3.3 %copy.44 = f32[64,32,2,64]{0,3,2,1:T(8,128)} copy(f32[64,32,2,64]{3,1,0,2:T(8,128)} %bitcast.60) | data formatting | bytes 2097152 | tf_op jit(solution)/shard_map/all_to_all | solution.py:83
  114.1 0.0 reduce-scatter.5.cloned.1.call-update
  114.1 0.0 copy-done.5
  114.1 0.0 copy-done.2
  114.1 0.2 convert_reduce_fusion
  114.3 33.9 %psum.15 = f32[128]{0:T(128)S(1)} all-reduce(f32[128]{0:T(128)S(1)} %convert_reduce_fusion), channel_id=1, replica_groups=mesh['grp'=2,'row'=8,'col'=2] {'row','col'}, use_global_device_ids=true, to_apply=%region_4.0 | all-reduce | flops 128 | bytes 1024 | tf_op jit(solution)/shard_map/psum | solution.py:85
  148.2 0.5 broadcast_multiply_fusion.1
  148.7 1.4 fusion.3
  150.1 10.0 %all-reduce.2.cloned.1.call-done = f32[1024,128]{1,0:T(8,128)} async-done(((f32[1024,128]{1,0:T(8,128)}), f32[1024,128]{1,0:T(8,128)}) %all-reduce.2.cloned.1.call-update) | async-done | bytes 524304 | tf_op jit(solution)/shard_map/psum | solution.py:85
  160.1 1.9 broadcast_multiply_fusion
  162.0 0.0 reduce-scatter.7.cloned.1.call-done
  162.0 1.1 reshape.38
  163.1 1.0 copy.45
  164.1 19.6 %reduce-scatter.5.cloned.1.call-done = f32[64,32,16]{0,2,1:T(8,128)} async-done(((f32[64,32,128]{0,2,1:T(8,128)}), f32[64,32,16]{0,2,1:T(8,128)}) %reduce-scatter.5.cloned.1.call-update) | async-done | bytes 131088 | tf_op jit(solution)/shard_map/reduce_scatter | solution.py:84
  (1 shorter events, 0.0 us)
Async XLA Ops:
  8.0 58.9 %copy-start = (bf16[1024,128]{1,0:T(8,128)(2,1)S(1)}, bf16[1024,128]{1,0:T(8,128)(2,1)}, u32[]{:S(2)}) copy-start(bf16[1024,128]{1,0:T(8,128)(2,1)} %param.7) | copy-start | bytes 786436
  45.1 7.5 %all-to-all-start = ((bf16[2,2,65536]{2,1,0:T(2,128)(2,1)}), bf16[2,2,65536]{2,1,0:T(2,128)(2,1)S(1)}, u32[]{:S(2)}, u32[]{:S(2)}) async-start(bf16[2,2,65536]{2,1,0:T(2,128)(2,1)} %reshape.39), calls=%async_computation | async-start | bytes 1048576 | tf_op jit(solution)/shard_map/all_to_all | solution.py:56
  48.6 111.6 %all-reduce.2.cloned.1.call-start = ((), (), s32[]{:S(2)}) async-start(), calls=%async_computation.5 | async-start | bytes 1048576 | tf_op jit(solution)/shard_map/psum | solution.py:85
  54.9 1.3 copy-start.3
  59.7 5.5 %copy-start.1 = (bf16[16,64,128]{2,1,0:T(8,128)(2,1)S(1)}, bf16[16,64,128]{2,1,0:T(8,128)(2,1)}, u32[]{:S(2)}) copy-start(bf16[16,64,128]{2,1,0:T(8,128)(2,1)} %param.9) | copy-start | bytes 786436
  66.8 95.2 %reduce-scatter.7.cloned.1.call-start = ((), (), s32[]{:S(2)}) async-start(), calls=%async_computation.6 | async-start | bytes 393216
  68.9 10.4 %copy-start.4 = (bf16[128,32,64,1]{0,2,1,3:T(8,128)(2,1)S(1)}, bf16[128,32,64,1]{0,2,1,3:T(8,128)(2,1)}, u32[]{:S(2)}) copy-start(bf16[128,32,64,1]{0,2,1,3:T(8,128)(2,1)} %copy-done.3) | copy-start | bytes 1572868
  87.8 95.8 %reduce-scatter.5.cloned.1.call-start = ((), (), s32[]{:S(2)}) async-start(), calls=%async_computation.4 | async-start | bytes 2359296 | tf_op jit(solution)/shard_map/reduce_scatter | solution.py:84
  108.3 5.8 %copy-start.5 = (bf16[128]{0:T(256)(128)(2,1)S(1)}, bf16[128]{0:T(256)(128)(2,1)}, u32[]{:S(2)}) copy-start(bf16[128]{0:T(256)(128)(2,1)} %param.8) | copy-start | bytes 772
  110.8 3.3 %copy-start.2 = (bf16[16,64,128]{2,1,0:T(8,128)(2,1)S(1)}, bf16[16,64,128]{2,1,0:T(8,128)(2,1)}, u32[]{:S(2)}) copy-start(bf16[16,64,128]{2,1,0:T(8,128)(2,1)} %param.9) | copy-start | bytes 786436
Sparse Core Ops, SparseCore 0:
  66.9 93.1 all-reduce.1
Sparse Core Ops, SparseCore 1:
  87.9 8.5 reduce-scatter.6
  114.2 69.4 reduce-scatter.4
where the time goes:
time: 192 us; the launch traced here: 191 us
  blocking collectives  76.1 us (40%)
  local copies, waits for them, and re-layouts  44.8 us (23%)
  waiting for transfers between devices  29.7 us (15%)
  between operations  15.7 us (8%)
  matrix products  13.6 us (7%)
  other arithmetic  7.47 us (4%)
  starting transfers between devices  3.8 us (2%)
    all_gather x1, blocking collectives, local(): gathered = lax.all_gather(alignment_right, 'row', axis=2, tiled=True)  34.6 us
    psum x1, blocking collectives, local(): weight_sum, bias_sum = lax.psum((weight_acc, bias_term), ('row', 'col'))  33.9 us
    reduce_scatter x1, waiting for transfers between devices, local(): lax.psum_scatter(returned, 'row', scatter_dimension=2, tiled=True)  19.6 us
    unnamed x22, local copies, waits for them, and re-layouts  16.3 us
    psum x1, waiting for transfers between devices, local(): weight_sum, bias_sum = lax.psum((weight_acc, bias_term), ('row', 'col'))  10 us
    reshape x1, local copies, waits for them, and re-layouts, pair_block(): grad_outer.astype(jnp.bfloat16)  6.38 us
    reshape x1, local copies, waits for them, and re-layouts, pair_block(): outer_tile = (outer_tile * inv_seqs).astype(jnp.bfloat16).reshape(row_cou...  5.52 us
    all_to_all x1, blocking collectives, local(): lax.all_to_all(cols_acc, 'col', split_axis=0, concat_axis=2, tiled=True)  5.36 us
  transfers between devices with their start and end apart: 4, of which 2 were waited for; matrix products, arithmetic and copies ran while one was open for 26% of the time, Pallas kernels for 0%

commit v1 on v0

v1 whole, which is shorter than its diff:
```python
import functools

import jax
import jax.numpy as jnp
from jax import lax
from jax.experimental import pallas as pl
from jax.experimental.pallas import tpu as pltpu
from jax.sharding import PartitionSpec as P

MESH = pl.DeviceIdType.MESH
F32, BF16 = jnp.float32, jnp.bfloat16


def dot(a, b, ca=1, cb=0):
    return lax.dot_general(a, b, (((ca,), (cb,)), ((), ())), preferred_element_type=F32)


def kernel(
    rows, own, left_ref, right_ref, w_ref, bias_ref, cot_ref,
    pair_ref, gl_ref, gr_ref, gw_ref, gb_ref,
    lbuf, rbuf, perm, lt, wt, bd, scr, grs, rs, os, gsend, gbuf,
    gacc, wsib, wsend, wr, agbuf, glacc, glsib, bsend, bbuf,
    lsem, rssem, rsem, gssem, gsem, wsem, wssem, wrsem, assem, asem, fsem, glsem, bssem, bsem,
):
    g, r, k = lax.axis_index("grp"), lax.axis_index("row"), lax.axis_index("col")
    sib = 1 - k
    half_s, wide = left_ref.shape
    ires = cot_ref.shape[0]
    chan = wide // ires
    d2n = chan // 2
    seqs = 2 * half_s
    inv_seqs = 1.0 / seqs
    owners = rows // 2
    per = 64 // ires
    blocks = owners // per
    kt, ol = r // owners, r % owners
    stride = rows // own
    lanes = d2n * 128

    def remote(src, dst, ss, rs_, row, col):
        return pltpu.make_async_remote_copy(
            src_ref=src, dst_ref=dst, send_sem=ss, recv_sem=rs_,
            device_id=(g, row, col), device_id_type=MESH)

    def landed(ref, sem):
        pltpu.make_async_copy(ref, ref, sem).wait()

    barrier = pltpu.get_barrier_semaphore()

    @pl.loop(1, 2 * rows)
    def _(t):
        q = (2 * r + k + t) % (2 * rows)
        pl.semaphore_signal(barrier, inc=1, device_id=(g, q // 2, q % 2), device_id_type=MESH)

    pl.semaphore_wait(barrier, 2 * rows - 1)

    left_copy = remote(left_ref, lbuf.at[k], lsem.at[0], lsem.at[1], r, sib)
    left_copy.start()

    def right_copy(t):
        return remote(right_ref, rbuf.at[ol, k], rssem.at[t], rsem.at[ol, k], (r + t) % rows, kt)

    @pl.when(kt == k)
    def _():
        pltpu.make_async_copy(right_ref, rbuf.at[ol, k], rsem.at[ol, k]).start()

    @pl.when(kt != k)
    def _():
        remote(right_ref, rbuf.at[ol, k], rssem.at[0], rsem.at[ol, k], r, sib).start()

    @pl.loop(1, rows)
    def _(t):
        right_copy(t).start()

    bsend[...] = jnp.broadcast_to(
        jnp.sum(cot_ref[...].astype(F32), axis=(0, 1)).reshape(1, -1), bsend.shape)

    def bias_copy(t):
        q = (2 * r + k + t) % (2 * rows)
        return remote(bsend, bbuf.at[2 * r + k], bssem.at[t], bsem.at[2 * r + k], q // 2, q % 2)

    @pl.loop(1, 2 * rows)
    def _(t):
        bias_copy(t).start()

    bbuf[2 * r + k] = bsend[...]
    lbuf[k] = left_ref[...]

    dd = 128 // ires
    pm = lax.broadcasted_iota(jnp.int32, perm.shape, 0)
    pn = lax.broadcasted_iota(jnp.int32, perm.shape, 1)
    goal = (pm % 128 // ires) * 64 + (pm // 128) * ires + pm % ires
    perm[...] = jnp.where(goal == pn, 1.0, 0.0).astype(BF16)
    wt[...] = w_ref[...].astype(F32).T.astype(BF16)
    bd[...] = jnp.zeros(bd.shape, BF16)

    def fill_bd(b):
        for i in range(ires):
            piece = cot_ref[i, pl.ds(pl.multiple_of(b * 64, 64), 64), :]
            bd[i * 128 : i * 128 + 64, 0:128] = piece
            bd[i * 128 + 64 : i * 128 + 128, 128:256] = piece

    def each_block(fn):
        if blocks == 1:
            fn(0)
        else:
            pl.loop(0, blocks)(fn)

    def grads(b):
        fill_bd(b)

        @pl.loop(0, ires // 2)
        def _(p):
            res = dot(w_ref[...], bd[pl.ds(pl.multiple_of(p * 256, 256), 256), :], 1, 1)
            for u in range(2):
                scr[u] = res[:, u * 128 : u * 128 + 128]
            for u in range(2):
                at = pl.multiple_of((2 * p + u) * chan, chan)
                for q in range(d2n):
                    grs[b, pl.ds(at, chan), q * 128 : q * 128 + 128] = scr[
                        u, pl.ds(q, chan, stride=d2n), :].astype(BF16)

    each_block(grads)

    left_copy.wait_recv()
    lm = lbuf[...].reshape(seqs, wide)
    lt[...] = lm.astype(F32).T.astype(BF16)

    def right_back(o, h):
        return remote(gsend.at[o, h], gbuf.at[r], gssem.at[o, h], gsem.at[r], k * owners + o, h)

    def right_terms(b):
        for q in range(lanes // 512):
            part = dot(lbuf[...].reshape(seqs, wide), grs[b, :, q * 512 : q * 512 + 512])
            part = dot(part.astype(BF16), perm[...], 1, 1).astype(BF16)
            for o in range(per):
                for h in range(2):
                    gsend[b * per + o, h, :, q * 128 : q * 128 + 128] = part[
                        h * half_s : (h + 1) * half_s, o * 128 : o * 128 + 128]

        @pl.loop(0, 2 * per)
        def _(x):
            o, h = b * per + (x // 2 + r) % per, x % 2
            mine = (k * owners + o == r) & (h == k)

            @pl.when(mine)
            def _():
                pltpu.make_async_copy(gsend.at[o, h], gbuf.at[r], gsem.at[r]).start()

            @pl.when(jnp.logical_not(mine))
            def _():
                right_back(o, h).start()

    each_block(right_terms)

    if blocks > 1:
        gacc[...] = jnp.zeros(gacc.shape, F32)
        glacc[...] = jnp.zeros(glacc.shape, F32)

    half_w = gacc.shape[1]

    def weight_half(hh):
        at = pl.ds(pl.multiple_of(hh * half_w, half_w), half_w)
        val = dot(os[at, :], bd[...])
        if blocks == 1:
            gacc[hh] = val
        else:
            gacc[hh] += val

    weight_copy = remote(gacc.at[sib], wsib, wsem.at[0], wsem.at[1], r, sib)
    lane = lax.broadcasted_iota(jnp.int32, (128, 128), 1)

    def forward(b):
        if blocks > 1:
            fill_bd(b)
        for o in range(per):
            for h in range(2):
                landed(rbuf.at[b * per + o, h], rsem.at[b * per + o, h])
        for q in range(lanes // 512):
            cat = jnp.concatenate(
                [rbuf[b * per + o, :, :, q * 128 : q * 128 + 128].reshape(seqs, 128)
                 for o in range(per)], axis=1)
            rs[:, q * 512 : q * 512 + 512] = dot(cat, perm[...]).astype(BF16)

        @pl.loop(0, d2n // 2)
        def _(p):
            res = dot(lt[...], rs[:, pl.ds(pl.multiple_of(p * 256, 256), 256)]) * inv_seqs
            for u in range(2):
                for i in range(ires):
                    scr[i, pl.ds(2 * p + u, chan, stride=d2n), :] = res[
                        i * chan : (i + 1) * chan, u * 128 : u * 128 + 128]

        for i in range(ires):
            os[:, i * 128 : i * 128 + 128] = scr[i].astype(BF16)

        weight_half(sib)
        if blocks == 1:
            weight_copy.start()
        weight_half(k)

        @pl.loop(0, ires // 2)
        def _(p):
            res = dot(wt[...], os[:, pl.ds(pl.multiple_of(p * 256, 256), 256)])
            for u in range(2):
                both = jnp.where(
                    lane < 64, res[0:128, u * 128 : u * 128 + 128],
                    res[128:256, u * 128 : u * 128 + 128]).T
                pair_ref[2 * p + u, pl.ds(pl.multiple_of(b * 64, 64), 64), :] = (
                    both[0:64] + both[64:128] + bias_ref[...].astype(F32)).astype(BF16)

        val = dot(rs[...], grs[b], 1, 1)
        for h in range(2):
            if blocks == 1:
                glacc[h] = val[h * half_s : (h + 1) * half_s]
            else:
                glacc[h] += val[h * half_s : (h + 1) * half_s]

    each_block(forward)
    if blocks > 1:
        weight_copy.start()
    gl_copy = remote(glacc.at[sib], glsib, glsem.at[0], glsem.at[1], r, sib)
    gl_copy.start()

    weight_copy.wait_recv()
    slab = half_w // own
    wsend[...] = (gacc[k] + wsib[...]).astype(BF16).reshape(wsend.shape)

    def weight_send(p):
        return remote(wsend.at[p], wr.at[r], wssem.at[p], wrsem.at[r], p * stride, k)

    @pl.loop(0, own)
    def _(t):
        p = (r // stride + t) % own

        @pl.when(p * stride == r)
        def _():
            pltpu.make_async_copy(wsend.at[p], wr.at[r], wrsem.at[r]).start()

        @pl.when(p * stride != r)
        def _():
            weight_send(p).start()

    total = jnp.zeros((half_s, wide), F32)
    if rows <= 8:
        for q in range(rows):
            landed(gbuf.at[q], gsem.at[q])
            total = total + gbuf[q].astype(F32)
        gr_ref[...] = total * inv_seqs
    else:
        gr_ref[...] = total

        @pl.loop(0, rows)
        def _(q):
            landed(gbuf.at[q], gsem.at[q])
            gr_ref[...] += gbuf[q].astype(F32) * inv_seqs

    inv_rows = 1.0 / (ires * rows)
    me = r // stride

    def share(t):
        return remote(agbuf.at[k, me], agbuf.at[k, me], assem.at[t], asem.at[k, me], (r + t) % rows, k)

    def pass_on(p):
        return remote(agbuf.at[k, p], agbuf.at[k, p], fsem.at[p], asem.at[k, p], r, sib)

    def own_slice():
        def add(q, acc):
            landed(wr.at[q], wrsem.at[q])
            return acc + wr[q].astype(F32)

        agbuf[k, me] = lax.fori_loop(0, rows, add, jnp.zeros((slab, 256), F32)) * inv_rows
        pl.loop(1, rows)(lambda t: share(t).start())
        pass_on(me).start()

    if stride == 1:
        own_slice()
    else:
        pl.when(r % stride == 0)(own_slice)

    gl_copy.wait_recv()
    gl_ref[...] = (glacc[k] + glsib[...]) * inv_seqs

    def add_bias(q, acc):
        @pl.when(q != 2 * r + k)
        def _():
            landed(bbuf.at[q], bsem.at[q])

        return acc + bbuf[q]

    gb_ref[...] = lax.fori_loop(0, 2 * rows, add_bias, jnp.zeros(bsend.shape, F32)) * inv_rows

    @pl.loop(0, own)
    def _(t):
        p = (me + t) % own

        @pl.when(p * stride != r)
        def _():
            landed(agbuf.at[k, p], asem.at[k, p])
            pass_on(p).start()

    @pl.loop(0, own)
    def _(p):
        landed(agbuf.at[sib, p], asem.at[sib, p])

    whole = agbuf[...].reshape(2 * half_w, 256)
    gw_ref[pl.ds(0, 2 * half_w, stride=2), :] = whole[:, 0:128]
    gw_ref[pl.ds(1, 2 * half_w, stride=2), :] = whole[:, 128:256]

    left_copy.wait_send()

    @pl.when(kt != k)
    def _():
        remote(right_ref, rbuf.at[ol, k], rssem.at[0], rsem.at[ol, k], r, sib).wait_send()

    pl.loop(1, rows)(lambda t: right_copy(t).wait_send())
    pl.loop(1, 2 * rows)(lambda t: bias_copy(t).wait_send())

    @pl.loop(0, 2 * owners)
    def _(x):
        o, h = x // 2, x % 2

        @pl.when(jnp.logical_not((k * owners + o == r) & (h == k)))
        def _():
            right_back(o, h).wait_send()

    weight_copy.wait_send()
    gl_copy.wait_send()

    @pl.loop(0, own)
    def _(p):
        @pl.when(p * stride != r)
        def _():
            weight_send(p).wait_send()

    def shared():
        pl.loop(1, rows)(lambda t: share(t).wait_send())

    if stride == 1:
        shared()
    else:
        pl.when(r % stride == 0)(shared)
    pl.loop(0, own)(lambda p: pass_on(p).wait_send())


def local(rows, alignment_left, alignment_right, weight, pairwise_bias, cotangent):
    half_s, chan, ires = alignment_left.shape
    wide = chan * ires
    pair_dim = weight.shape[1]
    d2n = chan // 2
    own = min(rows, 8)
    owners = rows // 2
    blocks = owners * ires // 64
    half_w = chan * d2n // 2
    left = jnp.transpose(alignment_left, (0, 2, 1)).reshape(half_s, wide)
    right = alignment_right.reshape(half_s, wide)
    w = weight.reshape(chan * d2n, 2 * pair_dim)
    vmem, dma = pltpu.VMEM, pltpu.SemaphoreType.DMA
    lanes = d2n * 128
    pair, gl, gr, gw, gb = pl.pallas_call(
        functools.partial(kernel, rows, own),
        out_shape=(
            jax.ShapeDtypeStruct(cotangent.shape, BF16),
            jax.ShapeDtypeStruct((half_s, wide), F32),
            jax.ShapeDtypeStruct((half_s, wide), F32),
            jax.ShapeDtypeStruct((chan * chan, pair_dim), F32),
            jax.ShapeDtypeStruct((8, pair_dim), F32),
        ),
        in_specs=[pl.BlockSpec(memory_space=vmem)] * 5,
        out_specs=tuple([pl.BlockSpec(memory_space=vmem)] * 5),
        scratch_shapes=[
            vmem((2, half_s, wide), BF16),
            vmem((owners, 2, half_s, wide), BF16),
            vmem((512, 512), BF16),
            vmem((wide, 2 * half_s), BF16),
            vmem((2 * pair_dim, chan * d2n), BF16),
            vmem((ires * 128, 2 * pair_dim), BF16),
            vmem((ires, chan * d2n, 128), F32),
            vmem((blocks, wide, lanes), BF16),
            vmem((2 * half_s, lanes), BF16),
            vmem((chan * d2n, ires * 128), BF16),
            vmem((owners, 2, half_s, wide), BF16),
            vmem((rows, half_s, wide), BF16),
            vmem((2, half_w, 2 * pair_dim), F32),
            vmem((half_w, 2 * pair_dim), F32),
            vmem((own, half_w // own, 2 * pair_dim), BF16),
            vmem((rows, half_w // own, 2 * pair_dim), BF16),
            vmem((2, own, half_w // own, 2 * pair_dim), F32),
            vmem((2, half_s, wide), F32),
            vmem((half_s, wide), F32),
            vmem((8, pair_dim), F32),
            vmem((2 * rows, 8, pair_dim), F32),
            dma((2,)), dma((rows,)), dma((owners, 2)), dma((owners, 2)), dma((rows,)),
            dma((2,)), dma((own,)), dma((rows,)), dma((rows,)), dma((2, own)), dma((own,)),
            dma((2,)), dma((2 * rows,)), dma((2 * rows,)),
        ],
        compiler_params=pltpu.CompilerParams(
            collective_id=0, has_side_effects=True, vmem_limit_bytes=58 * 2**20),
    )(left, right, w, pairwise_bias.reshape(1, pair_dim), cotangent)
    gl = jnp.transpose(gl.reshape(half_s, ires, chan), (0, 2, 1))
    return pair, gl, gr.reshape(half_s, chan, ires), gw, gb[0]


def solution(mesh):
    in_specs = (
        P("col", None, ("grp", "row")),
        P("col", None, ("grp", "row")),
        P(),
        P(),
        P(("grp", "row"), "col", None),
    )
    out_specs = (
        P(("grp", "row"), "col", None),
        P("col", None, ("grp", "row")),
        P("col", None, ("grp", "row")),
        P("grp", None),
        P("grp"),
    )
    return jax.shard_map(
        functools.partial(local, mesh.shape["row"]), mesh=mesh,
        in_specs=in_specs, out_specs=out_specs, check_vma=False)
```

time: 192 us -> 54.9 us (0.29)
  blocking collectives: 76.1 us -> 0 us
  Pallas kernels: 0 us -> 44.8 us
  local copies, waits for them, and re-layouts: 44.8 us -> 8.88 us
  waiting for transfers between devices: 29.7 us -> 0 us
  between operations: 15.7 us -> 0.69 us
  matrix products: 13.6 us -> 0 us
  other arithmetic: 7.47 us -> 0 us
  starting transfers between devices: 3.8 us -> 0 us
    pallas_call x0 -> x1, Pallas kernels: none -> 44.8 us  [local(): pl.pallas_call(functools.partial(kernel, rows, own), out_shape=(jax.Shape...]
    all_gather x2 -> x0, blocking collectives: 36.8 us -> none  [the longest x1 34.6 us: local(): gathered = lax.all_gather(alignment_right, 'row', axis=2, tiled=True)]
    psum x1 -> x0, blocking collectives: 33.9 us -> none  [local(): weight_sum, bias_sum = lax.psum((weight_acc, bias_term), ('row', 'col'))]
    reduce_scatter x1 -> x0, waiting for transfers between devices: 19.6 us -> none  [local(): lax.psum_scatter(returned, 'row', scatter_dimension=2, tiled=True)]
    unnamed x22 -> x13, local copies, waits for them, and re-layouts: 16.3 us -> 2.57 us
    dot_general x6 -> x0, matrix products: 13.6 us -> none  [the longest x1 3.82 us: pair_block(): jnp.einsum('ijcd,sdj->sci', grad_outer, cols_part, preferred_element_type...]
    psum x1 -> x0, waiting for transfers between devices: 10 us -> none  [local(): weight_sum, bias_sum = lax.psum((weight_acc, bias_term), ('row', 'col'))]
    reshape x2 -> x3, local copies, waits for them, and re-layouts: 11.9 us -> 3.23 us  [the longest x1 1.78 us: local(): w = weight.reshape(chan * d2n, 2 * pair_dim)]
  transfers between devices with their start and end apart: 4 -> 0, of which waited for: 2 -> 0; matrix products, arithmetic and copies ran while one was open for 26% -> 0% of each run, Pallas kernels for 0% -> 0%
where the time goes in v1:
time: 54.9 us; the launch traced here: 54.3 us
  Pallas kernels  44.8 us (82%)
  local copies, waits for them, and re-layouts  8.88 us (16%)
  between operations  0.69 us (1%)
    pallas_call x1, Pallas kernels, local(): pl.pallas_call(functools.partial(kernel, rows, own), out_shape=(jax.Shape...  44.8 us
    unnamed x13, local copies, waits for them, and re-layouts  2.57 us
    pallas_call x2, local copies, waits for them, and re-layouts, local(): pl.pallas_call(functools.partial(kernel, rows, own), out_shape=(jax.Shape...  1.86 us
    reshape x1, local copies, waits for them, and re-layouts, local(): w = weight.reshape(chan * d2n, 2 * pair_dim)  1.78 us
    squeeze x1, local copies, waits for them, and re-layouts, local(): return (pair, gl, gr.reshape(half_s, chan, ires), gw, gb[0])  1.18 us

profile of v1, /device:TPU:0, one launch (start us, length us, event | category | flops | bytes accessed | tf_op | source)
XLA Modules:
  0.0 54.3 jit_solution(4060100739661139322)
XLA Ops:
  0.6 0.0 copy-start.4
  0.6 1.8 %reshape.30.w_ref = bf16[512,256]{1,0:T(8,128)(2,1)} reshape(bf16[1024,128]{1,0:T(8,128)(2,1)} %param.7) | data formatting | bytes 524288 | tf_op jit(solution)/shard_map/reshape | solution.py:356
  2.4 0.0 copy-done.4
  2.5 0.0 copy-start.3
  2.5 0.7 %copy.15.left_ref = bf16[64,512]{1,0:T(8,128)(2,1)} copy(bf16[64,512]{0,1:T(8,128)(2,1)S(1)} %bitcast.11) | data formatting | bytes 131072 | tf_op jit(solution)/shard_map/reshape | solution.py:354
  3.2 0.2 copy-done.3
  3.4 0.7 %copy.16.right_ref = bf16[64,512]{1,0:T(8,128)(2,1)} copy(bf16[64,512]{0,1:T(8,128)(2,1)S(1)} %bitcast.13) | data formatting | bytes 131072 | tf_op jit(solution)/shard_map/reshape | solution.py:355
  4.1 44.8 %shard_map.92 = (bf16[16,64,128]{2,1,0:T(8,128)(2,1)}, f32[64,512]{1,0:T(8,128)}, f32[64,512]{1,0:T(8,128)}, f32[1024,128]{1,0:T(8,128)}, f32[8,128]{1,0:T(8,128)}) custom-call(bf16[64,512]{1,0:T(8,128)(2,1)} %copy.15.left_ref, bf16[64,512]{1,0:T(8,128)(2,1)} %copy.16.right_ref, bf16[512,256]{1,0:T(8,128)(2,1)} %reshape.30.w_ref, bf16[1,128]{1,0:T(2,128)(2,1)} %bitcast.15, ...), custom_call_target="tpu_custom_call" | custom-call | tf_op jit(solution)/shard_map/pallas_call | solution.py:359
  48.9 1.0 %copy.17 = f32[64,512]{0,1:T(8,128)S(1)} copy(f32[64,512]{1,0:T(8,128)} %get-tuple-element.11) | data formatting | bytes 262144 | tf_op jit(solution)/shard_map/pallas_call | solution.py:359
  49.9 0.0 copy-start.2
  49.9 0.0 copy-start.1
  49.9 0.9 %copy.19 = f32[64,32,16]{0,2,1:T(8,128)} copy(f32[64,32,16]{0,1,2:T(8,128)S(1)} %bitcast.10) | data formatting | bytes 262144
  50.8 0.0 copy-start
  50.8 0.0 copy-done.2
  50.8 0.8 %copy.18 = f32[64,512]{0,1:T(8,128)} copy(f32[64,512]{1,0:T(8,128)S(1)} %copy-done.2) | data formatting | bytes 262144 | tf_op jit(solution)/shard_map/pallas_call | solution.py:359
  51.7 1.2 %slice_bitcast_fusion = f32[128]{0:T(128)} fusion(f32[8,128]{1,0:T(8,128)} %get-tuple-element.14), kind=kLoop, calls=%fused_computation | loop fusion | bytes 1024 | tf_op jit(solution)/shard_map/squeeze | solution.py:400
  52.8 0.0 copy-done.1
  52.8 0.7 %copy.22 = bf16[16,64,128]{2,1,0:T(8,128)(2,1)} copy(bf16[16,64,128]{2,1,0:T(8,128)(2,1)S(1)} %copy-done.1) | data formatting | bytes 524288
  53.5 0.0 copy-done
  53.6 0.8 %copy.23 = f32[1024,128]{1,0:T(8,128)} copy(f32[1024,128]{1,0:T(8,128)S(1)} %copy-done) | data formatting | bytes 1048576
  (1 shorter events, 0.0 us)
Async XLA Ops:
  0.6 1.8 %copy-start.4 = (bf16[64,32,16]{0,2,1:T(8,128)(2,1)S(1)}, bf16[64,32,16]{0,2,1:T(8,128)(2,1)}, u32[]{:S(2)}) copy-start(bf16[64,32,16]{0,2,1:T(8,128)(2,1)} %param.5) | copy-start | bytes 196612
  2.5 0.9 %copy-start.3 = (bf16[64,32,16]{0,2,1:T(8,128)(2,1)S(1)}, bf16[64,32,16]{0,2,1:T(8,128)(2,1)}, u32[]{:S(2)}) copy-start(bf16[64,32,16]{0,2,1:T(8,128)(2,1)} %param.6) | copy-start | bytes 196612
  49.9 0.9 %copy-start.2 = (f32[64,512]{1,0:T(8,128)S(1)}, f32[64,512]{1,0:T(8,128)}, u32[]{:S(2)}) copy-start(f32[64,512]{1,0:T(8,128)} %get-tuple-element.12) | copy-start | bytes 393220
  49.9 2.9 %copy-start.1 = (bf16[16,64,128]{2,1,0:T(8,128)(2,1)S(1)}, bf16[16,64,128]{2,1,0:T(8,128)(2,1)}, u32[]{:S(2)}) copy-start(bf16[16,64,128]{2,1,0:T(8,128)(2,1)} %get-tuple-element.30) | copy-start | bytes 786436
  50.8 2.8 %copy-start = (f32[1024,128]{1,0:T(8,128)S(1)}, f32[1024,128]{1,0:T(8,128)}, u32[]{:S(2)}) copy-start(f32[1024,128]{1,0:T(8,128)} %get-tuple-element.33) | copy-start | bytes 1572868

commit v2 on v1

--- a/solution.py
+++ b/solution.py
@@ -18,13 +18,13 @@
 def kernel(
     rows, own, left_ref, right_ref, w_ref, bias_ref, cot_ref,
     pair_ref, gl_ref, gr_ref, gw_ref, gb_ref,
-    lbuf, rbuf, perm, lt, wt, bd, scr, grs, rs, os, gsend, gbuf,
+    rsend, lsend, perm2, wf, w2, gls, lbuf, rbuf, perm, lt, wt, bd, scr, grs, rs, os, gsend, gbuf,
     gacc, wsib, wsend, wr, agbuf, glacc, glsib, bsend, bbuf,
     lsem, rssem, rsem, gssem, gsem, wsem, wssem, wrsem, assem, asem, fsem, glsem, bssem, bsem,
 ):
     g, r, k = lax.axis_index("grp"), lax.axis_index("row"), lax.axis_index("col")
     sib = 1 - k
-    half_s, wide = left_ref.shape
+    wide, half_s = left_ref.shape
     ires = cot_ref.shape[0]
     chan = wide // ires
     d2n = chan // 2
@@ -52,26 +52,31 @@
         q = (2 * r + k + t) % (2 * rows)
         pl.semaphore_signal(barrier, inc=1, device_id=(g, q // 2, q % 2), device_id_type=MESH)
 
+    rsend[...] = right_ref[...].astype(F32).T.astype(BF16)
     pl.semaphore_wait(barrier, 2 * rows - 1)
 
-    left_copy = remote(left_ref, lbuf.at[k], lsem.at[0], lsem.at[1], r, sib)
-    left_copy.start()
-
     def right_copy(t):
-        return remote(right_ref, rbuf.at[ol, k], rssem.at[t], rsem.at[ol, k], (r + t) % rows, kt)
+        return remote(rsend, rbuf.at[ol, k], rssem.at[t], rsem.at[ol, k], (r + t) % rows, kt)
 
     @pl.when(kt == k)
     def _():
-        pltpu.make_async_copy(right_ref, rbuf.at[ol, k], rsem.at[ol, k]).start()
+        pltpu.make_async_copy(rsend, rbuf.at[ol, k], rsem.at[ol, k]).start()
 
     @pl.when(kt != k)
     def _():
-        remote(right_ref, rbuf.at[ol, k], rssem.at[0], rsem.at[ol, k], r, sib).start()
+        remote(rsend, rbuf.at[ol, k], rssem.at[0], rsem.at[ol, k], r, sib).start()
 
     @pl.loop(1, rows)
     def _(t):
         right_copy(t).start()
 
+    pm = lax.broadcasted_iota(jnp.int32, (wide, wide), 0)
+    pn = lax.broadcasted_iota(jnp.int32, (wide, wide), 1)
+    perm2[...] = jnp.where((pm % ires) * chan + pm // ires == pn, 1.0, 0.0).astype(BF16)
+    lsend[...] = dot(left_ref[...], perm2[...], 0, 0).astype(BF16)
+    left_copy = remote(lsend, lbuf.at[k], lsem.at[0], lsem.at[1], r, sib)
+    left_copy.start()
+
     bsend[...] = jnp.broadcast_to(
         jnp.sum(cot_ref[...].astype(F32), axis=(0, 1)).reshape(1, -1), bsend.shape)
 
@@ -84,14 +89,18 @@
         bias_copy(t).start()
 
     bbuf[2 * r + k] = bsend[...]
-    lbuf[k] = left_ref[...]
+    lbuf[k] = lsend[...]
 
     dd = 128 // ires
     pm = lax.broadcasted_iota(jnp.int32, perm.shape, 0)
     pn = lax.broadcasted_iota(jnp.int32, perm.shape, 1)
     goal = (pm % 128 // ires) * 64 + (pm // 128) * ires + pm % ires
     perm[...] = jnp.where(goal == pn, 1.0, 0.0).astype(BF16)
-    wt[...] = w_ref[...].astype(F32).T.astype(BF16)
+    wf[...] = w_ref[...].astype(F32)
+    for u in range(2):
+        part = wf[pl.ds(u, chan * d2n, stride=2), :]
+        w2[:, u * 128 : u * 128 + 128] = part.astype(BF16)
+        wt[u * 128 : u * 128 + 128, :] = part.T.astype(BF16)
     bd[...] = jnp.zeros(bd.shape, BF16)
 
     def fill_bd(b):
@@ -111,7 +120,7 @@
 
         @pl.loop(0, ires // 2)
         def _(p):
-            res = dot(w_ref[...], bd[pl.ds(pl.multiple_of(p * 256, 256), 256), :], 1, 1)
+            res = dot(w2[...], bd[pl.ds(pl.multiple_of(p * 256, 256), 256), :], 1, 1)
             for u in range(2):
                 scr[u] = res[:, u * 128 : u * 128 + 128]
             for u in range(2):
@@ -245,14 +254,14 @@
         for q in range(rows):
             landed(gbuf.at[q], gsem.at[q])
             total = total + gbuf[q].astype(F32)
-        gr_ref[...] = total * inv_seqs
+        gr_ref[...] = (total * inv_seqs).T
     else:
-        gr_ref[...] = total
+        gr_ref[...] = total.T
 
         @pl.loop(0, rows)
         def _(q):
             landed(gbuf.at[q], gsem.at[q])
-            gr_ref[...] += gbuf[q].astype(F32) * inv_seqs
+            gr_ref[...] += (gbuf[q].astype(F32) * inv_seqs).T
 
     inv_rows = 1.0 / (ires * rows)
     me = r // stride
@@ -278,7 +287,9 @@
         pl.when(r % stride == 0)(own_slice)
 
     gl_copy.wait_recv()
-    gl_ref[...] = (glacc[k] + glsib[...]) * inv_seqs
+    gls[...] = ((glacc[k] + glsib[...]) * inv_seqs).T
+    for i in range(ires):
+        gl_ref[pl.ds(i, chan, stride=ires), :] = gls[i * chan : (i + 1) * chan, :]
 
     def add_bias(q, acc):
         @pl.when(q != 2 * r + k)
@@ -287,7 +298,8 @@
 
         return acc + bbuf[q]
 
-    gb_ref[...] = lax.fori_loop(0, 2 * rows, add_bias, jnp.zeros(bsend.shape, F32)) * inv_rows
+    bias_sum = lax.fori_loop(0, 2 * rows, add_bias, jnp.zeros(bsend.shape, F32)) * inv_rows
+    gb_ref[...] = bias_sum[0:1, :]
 
     @pl.loop(0, own)
     def _(t):
@@ -310,7 +322,7 @@
 
     @pl.when(kt != k)
     def _():
-        remote(right_ref, rbuf.at[ol, k], rssem.at[0], rsem.at[ol, k], r, sib).wait_send()
+        remote(rsend, rbuf.at[ol, k], rssem.at[0], rsem.at[ol, k], r, sib).wait_send()
 
     pl.loop(1, rows)(lambda t: right_copy(t).wait_send())
     pl.loop(1, 2 * rows)(lambda t: bias_copy(t).wait_send())
@@ -351,23 +363,28 @@
     owners = rows // 2
     blocks = owners * ires // 64
     half_w = chan * d2n // 2
-    left = jnp.transpose(alignment_left, (0, 2, 1)).reshape(half_s, wide)
-    right = alignment_right.reshape(half_s, wide)
-    w = weight.reshape(chan * d2n, 2 * pair_dim)
+    left = jnp.transpose(alignment_left, (1, 2, 0)).reshape(wide, half_s)
+    right = jnp.transpose(alignment_right, (1, 2, 0)).reshape(wide, half_s)
     vmem, dma = pltpu.VMEM, pltpu.SemaphoreType.DMA
     lanes = d2n * 128
     pair, gl, gr, gw, gb = pl.pallas_call(
         functools.partial(kernel, rows, own),
         out_shape=(
             jax.ShapeDtypeStruct(cotangent.shape, BF16),
-            jax.ShapeDtypeStruct((half_s, wide), F32),
-            jax.ShapeDtypeStruct((half_s, wide), F32),
+            jax.ShapeDtypeStruct((wide, half_s), F32),
+            jax.ShapeDtypeStruct((wide, half_s), F32),
             jax.ShapeDtypeStruct((chan * chan, pair_dim), F32),
-            jax.ShapeDtypeStruct((8, pair_dim), F32),
+            jax.ShapeDtypeStruct((1, pair_dim), F32),
         ),
         in_specs=[pl.BlockSpec(memory_space=vmem)] * 5,
         out_specs=tuple([pl.BlockSpec(memory_space=vmem)] * 5),
         scratch_shapes=[
+            vmem((half_s, wide), BF16),
+            vmem((half_s, wide), BF16),
+            vmem((wide, wide), BF16),
+            vmem((chan * chan, pair_dim), F32),
+            vmem((chan * d2n, 2 * pair_dim), BF16),
+            vmem((wide, half_s), F32),
             vmem((2, half_s, wide), BF16),
             vmem((owners, 2, half_s, wide), BF16),
             vmem((512, 512), BF16),
@@ -395,9 +412,9 @@
         ],
         compiler_params=pltpu.CompilerParams(
             collective_id=0, has_side_effects=True, vmem_limit_bytes=58 * 2**20),
-    )(left, right, w, pairwise_bias.reshape(1, pair_dim), cotangent)
-    gl = jnp.transpose(gl.reshape(half_s, ires, chan), (0, 2, 1))
-    return pair, gl, gr.reshape(half_s, chan, ires), gw, gb[0]
+    )(left, right, weight, pairwise_bias.reshape(1, pair_dim), cotangent)
+    gl, gr = (jnp.transpose(x.reshape(chan, ires, half_s), (2, 0, 1)) for x in (gl, gr))
+    return pair, gl, gr, gw, gb.reshape(pair_dim)
 
 
 def solution(mesh):

time: 54.9 us -> 50.6 us (0.922)
  local copies, waits for them, and re-layouts: 8.88 us -> 4.45 us
    reshape x3 -> x0, local copies, waits for them, and re-layouts: 3.23 us -> none  [the longest x1 1.78 us: local(): w = weight.reshape(chan * d2n, 2 * pair_dim)]
    unnamed x13, local copies, waits for them, and re-layouts: 2.57 us -> 4.45 us
    pallas_call x2 -> x0, local copies, waits for them, and re-layouts: 1.86 us -> none  [local(): pl.pallas_call(functools.partial(kernel, rows, own), out_shape=(jax.Shape...]
    squeeze x1 -> x0, local copies, waits for them, and re-layouts: 1.18 us -> none  [local(): return (pair, gl, gr.reshape(half_s, chan, ires), gw, gb[0])]
where the time goes in v2:
time: 50.6 us; the launch traced here: 50.1 us
  Pallas kernels  45 us (89%)
  local copies, waits for them, and re-layouts  4.45 us (9%)
  between operations  0.66 us (1%)
    pallas_call x1, Pallas kernels, local(): pl.pallas_call(functools.partial(kernel, rows, own), out_shape=(jax.Shape...  45 us
    unnamed x13, local copies, waits for them, and re-layouts  4.45 us

profile of v2, /device:TPU:0, one launch (start us, length us, event | category | flops | bytes accessed | tf_op | source)
XLA Modules:
  0.0 50.1 jit_solution(5636107550637573336)
XLA Ops:
  0.6 45.0 %shard_map.92 = (bf16[16,64,128]{2,1,0:T(8,128)(2,1)}, f32[512,64]{1,0:T(8,128)}, f32[512,64]{1,0:T(8,128)}, f32[1024,128]{1,0:T(8,128)}, f32[1,128]{1,0:T(1,128)}) custom-call(bf16[512,64]{1,0:T(8,128)(2,1)} %bitcast.16, bf16[512,64]{1,0:T(8,128)(2,1)} %bitcast.17, bf16[1024,128]{1,0:T(8,128)(2,1)} %w_ref.1, bf16[1,128]{1,0:T(2,128)(2,1)} %bitcast.18, ...), custom_call_target="tpu_custom_call" | custom-call | tf_op jit(solution)/shard_map/pallas_call | solution.py:370
  45.6 0.0 copy-start.2
  45.6 0.0 copy-start.1
  45.6 1.7 %copy.15 = bf16[16,64,128]{2,1,0:T(8,128)(2,1)} copy(bf16[16,64,128]{2,1,0:T(8,128)(2,1)} %get-tuple-element.20) | data formatting | bytes 524288
  47.3 0.0 copy-done.2
  47.3 0.0 copy-start
  47.3 0.7 %copy.16 = f32[64,32,16]{0,2,1:T(8,128)} copy(f32[64,32,16]{0,2,1:T(8,128)S(1)} %bitcast.15) | data formatting | bytes 262144
  48.0 0.0 copy-done.1
  48.1 0.7 %copy.17 = f32[64,32,16]{0,2,1:T(8,128)} copy(f32[64,32,16]{0,2,1:T(8,128)S(1)} %bitcast.14) | data formatting | bytes 262144
  48.8 0.0 copy-done
  48.8 0.0 copy-start.3
  48.8 0.8 %copy.18 = f32[1024,128]{1,0:T(8,128)} copy(f32[1024,128]{1,0:T(8,128)S(1)} %copy-done) | data formatting | bytes 1048576
  49.6 0.0 copy-done.3
  49.6 0.5 %copy.19 = f32[128]{0:T(128)} copy(f32[128]{0:T(128)S(1)} %bitcast.19) | data formatting | bytes 1024
Async XLA Ops:
  45.6 1.7 %copy-start.2 = (f32[512,64]{1,0:T(8,128)S(1)}, f32[512,64]{1,0:T(8,128)}, u32[]{:S(2)}) copy-start(f32[512,64]{1,0:T(8,128)} %get-tuple-element.11) | copy-start | bytes 393220
  45.6 2.4 %copy-start.1 = (f32[512,64]{1,0:T(8,128)S(1)}, f32[512,64]{1,0:T(8,128)}, u32[]{:S(2)}) copy-start(f32[512,64]{1,0:T(8,128)} %get-tuple-element.12) | copy-start | bytes 393220
  47.3 1.4 %copy-start = (f32[1024,128]{1,0:T(8,128)S(1)}, f32[1024,128]{1,0:T(8,128)}, u32[]{:S(2)}) copy-start(f32[1024,128]{1,0:T(8,128)} %get-tuple-element.23) | copy-start | bytes 1572868
  48.8 0.8 %copy-start.3 = (f32[1,128]{1,0:T(1,128)S(1)}, f32[1,128]{1,0:T(1,128)}, u32[]{:S(2)}) copy-start(f32[1,128]{1,0:T(1,128)} %get-tuple-element.14) | copy-start | bytes 1540

commit v3 on v2

--- a/solution.py
+++ b/solution.py
@@ -20,7 +20,7 @@
     pair_ref, gl_ref, gr_ref, gw_ref, gb_ref,
     rsend, lsend, perm2, wf, w2, gls, lbuf, rbuf, perm, lt, wt, bd, scr, grs, rs, os, gsend, gbuf,
     gacc, wsib, wsend, wr, agbuf, glacc, glsib, bsend, bbuf,
-    lsem, rssem, rsem, gssem, gsem, wsem, wssem, wrsem, assem, asem, fsem, glsem, bssem, bsem,
+    lsem, rssem, rsem, gssem, gsem, wsem, wssem, wrsem, assem, asem, fsem, glsem, bssem, bsem, hsem, gmid, gmsem, gm2sem,
 ):
     g, r, k = lax.axis_index("grp"), lax.axis_index("row"), lax.axis_index("col")
     sib = 1 - k
@@ -34,6 +34,9 @@
     per = 64 // ires
     blocks = owners // per
     kt, ol = r // owners, r % owners
+    y = r % 2
+    peer = r + 1 - 2 * y
+    cols = rows // 2
     stride = rows // own
     lanes = d2n * 128
 
@@ -56,7 +59,7 @@
     pl.semaphore_wait(barrier, 2 * rows - 1)
 
     def right_copy(t):
-        return remote(rsend, rbuf.at[ol, k], rssem.at[t], rsem.at[ol, k], (r + t) % rows, kt)
+        return remote(rsend, rbuf.at[ol, k], rssem.at[t], rsem.at[ol, k], (r + 2 * t) % rows, kt)
 
     @pl.when(kt == k)
     def _():
@@ -66,13 +69,35 @@
     def _():
         remote(rsend, rbuf.at[ol, k], rssem.at[0], rsem.at[ol, k], r, sib).start()
 
-    @pl.loop(1, rows)
+    peer_copy = remote(rsend, rbuf.at[ol, k], rssem.at[cols], rsem.at[ol, k], peer, kt)
+    peer_copy.start()
+
+    @pl.loop(1, cols)
     def _(t):
         right_copy(t).start()
 
+    def hand_on(x):
+        o, h = 2 * (x // 2) + y, x % 2
+        return remote(rbuf.at[o, h], rbuf.at[o, h], hsem.at[x], rsem.at[o, h], peer, k)
+
+    def not_mine(x):
+        return k * owners + 2 * (x // 2) + y != r
+
+    def hand_all():
+        @pl.loop(0, owners)
+        def _(x):
+            o, h = 2 * (x // 2) + y, x % 2
+            landed(rbuf.at[o, h], rsem.at[o, h])
+
+            @pl.when(not_mine(x))
+            def _():
+                hand_on(x).start()
+
+    ibits, dbits = ires.bit_length() - 1, (128 // ires).bit_length() - 1
     pm = lax.broadcasted_iota(jnp.int32, (wide, wide), 0)
     pn = lax.broadcasted_iota(jnp.int32, (wide, wide), 1)
-    perm2[...] = jnp.where((pm % ires) * chan + pm // ires == pn, 1.0, 0.0).astype(BF16)
+    goal = (pm & (ires - 1)) * chan + (pm >> ibits)
+    perm2[...] = jnp.where(goal == pn, 1.0, 0.0).astype(BF16)
     lsend[...] = dot(left_ref[...], perm2[...], 0, 0).astype(BF16)
     left_copy = remote(lsend, lbuf.at[k], lsem.at[0], lsem.at[1], r, sib)
     left_copy.start()
@@ -91,10 +116,9 @@
     bbuf[2 * r + k] = bsend[...]
     lbuf[k] = lsend[...]
 
-    dd = 128 // ires
     pm = lax.broadcasted_iota(jnp.int32, perm.shape, 0)
     pn = lax.broadcasted_iota(jnp.int32, perm.shape, 1)
-    goal = (pm % 128 // ires) * 64 + (pm // 128) * ires + pm % ires
+    goal = ((pm >> ibits) & (2**dbits - 1)) * 64 + (pm >> 7) * ires + (pm & (ires - 1))
     perm[...] = jnp.where(goal == pn, 1.0, 0.0).astype(BF16)
     wf[...] = w_ref[...].astype(F32)
     for u in range(2):
@@ -130,13 +154,19 @@
                         u, pl.ds(q, chan, stride=d2n), :].astype(BF16)
 
     each_block(grads)
+    hand_all()
 
     left_copy.wait_recv()
     lm = lbuf[...].reshape(seqs, wide)
     lt[...] = lm.astype(F32).T.astype(BF16)
 
     def right_back(o, h):
-        return remote(gsend.at[o, h], gbuf.at[r], gssem.at[o, h], gsem.at[r], k * owners + o, h)
+        return remote(
+            gsend.at[o, h], gbuf.at[r // 2], gssem.at[o, h], gsem.at[r // 2], k * owners + o, h)
+
+    def pair_send(x):
+        o, h = 2 * (x // 2) + 1 - y, x % 2
+        return remote(gsend.at[o, h], gmid.at[x], gm2sem.at[x], gmsem.at[x], peer, k)
 
     def right_terms(b):
         for q in range(lanes // 512):
@@ -147,18 +177,9 @@
                     gsend[b * per + o, h, :, q * 128 : q * 128 + 128] = part[
                         h * half_s : (h + 1) * half_s, o * 128 : o * 128 + 128]
 
-        @pl.loop(0, 2 * per)
+        @pl.loop(0, per)
         def _(x):
-            o, h = b * per + (x // 2 + r) % per, x % 2
-            mine = (k * owners + o == r) & (h == k)
-
-            @pl.when(mine)
-            def _():
-                pltpu.make_async_copy(gsend.at[o, h], gbuf.at[r], gsem.at[r]).start()
-
-            @pl.when(jnp.logical_not(mine))
-            def _():
-                right_back(o, h).start()
+            pair_send(b * per + x).start()
 
     each_block(right_terms)
 
@@ -182,14 +203,19 @@
     def forward(b):
         if blocks > 1:
             fill_bd(b)
-        for o in range(per):
-            for h in range(2):
-                landed(rbuf.at[b * per + o, h], rsem.at[b * per + o, h])
+        @pl.loop(0, per)
+        def _(x):
+            o, h = b * per + 2 * (x // 2) + 1 - y, x % 2
+            landed(rbuf.at[o, h], rsem.at[o, h])
+
         for q in range(lanes // 512):
             cat = jnp.concatenate(
                 [rbuf[b * per + o, :, :, q * 128 : q * 128 + 128].reshape(seqs, 128)
                  for o in range(per)], axis=1)
             rs[:, q * 512 : q * 512 + 512] = dot(cat, perm[...]).astype(BF16)
+
+        if blocks == 1:
+            pl.loop(0, owners)(right_sums)
 
         @pl.loop(0, d2n // 2)
         def _(p):
@@ -224,6 +250,22 @@
             else:
                 glacc[h] += val[h * half_s : (h + 1) * half_s]
 
+    def right_sums(x):
+        o, h = 2 * (x // 2) + y, x % 2
+        landed(gmid.at[x], gmsem.at[x])
+        gsend[o, h] = (gsend[o, h].astype(F32) + gmid[x].astype(F32)).astype(BF16)
+        mine = (k * owners + o == r) & (h == k)
+
+        @pl.when(mine)
+        def _():
+            pltpu.make_async_copy(gsend.at[o, h], gbuf.at[r // 2], gsem.at[r // 2]).start()
+
+        @pl.when(jnp.logical_not(mine))
+        def _():
+            right_back(o, h).start()
+
+    if blocks > 1:
+        pl.loop(0, owners)(right_sums)
     each_block(forward)
     if blocks > 1:
         weight_copy.start()
@@ -251,14 +293,14 @@
 
     total = jnp.zeros((half_s, wide), F32)
     if rows <= 8:
-        for q in range(rows):
+        for q in range(cols):
             landed(gbuf.at[q], gsem.at[q])
             total = total + gbuf[q].astype(F32)
         gr_ref[...] = (total * inv_seqs).T
     else:
         gr_ref[...] = total.T
 
-        @pl.loop(0, rows)
+        @pl.loop(0, cols)
         def _(q):
             landed(gbuf.at[q], gsem.at[q])
             gr_ref[...] += (gbuf[q].astype(F32) * inv_seqs).T
@@ -277,7 +319,8 @@
             landed(wr.at[q], wrsem.at[q])
             return acc + wr[q].astype(F32)
 
-        agbuf[k, me] = lax.fori_loop(0, rows, add, jnp.zeros((slab, 256), F32)) * inv_rows
+        mean = lax.fori_loop(0, rows, add, jnp.zeros((slab, 256), F32)) * inv_rows
+        agbuf[k, me] = mean.astype(BF16)
         pl.loop(1, rows)(lambda t: share(t).start())
         pass_on(me).start()
 
@@ -314,7 +357,7 @@
     def _(p):
         landed(agbuf.at[sib, p], asem.at[sib, p])
 
-    whole = agbuf[...].reshape(2 * half_w, 256)
+    whole = agbuf[...].astype(F32).reshape(2 * half_w, 256)
     gw_ref[pl.ds(0, 2 * half_w, stride=2), :] = whole[:, 0:128]
     gw_ref[pl.ds(1, 2 * half_w, stride=2), :] = whole[:, 128:256]
 
@@ -324,12 +367,22 @@
     def _():
         remote(rsend, rbuf.at[ol, k], rssem.at[0], rsem.at[ol, k], r, sib).wait_send()
 
-    pl.loop(1, rows)(lambda t: right_copy(t).wait_send())
+    pl.loop(1, cols)(lambda t: right_copy(t).wait_send())
+    peer_copy.wait_send()
+
+    @pl.loop(0, owners)
+    def _(x):
+        @pl.when(not_mine(x))
+        def _():
+            hand_on(x).wait_send()
+
+        pair_send(x).wait_send()
+
     pl.loop(1, 2 * rows)(lambda t: bias_copy(t).wait_send())
 
-    @pl.loop(0, 2 * owners)
+    @pl.loop(0, owners)
     def _(x):
-        o, h = x // 2, x % 2
+        o, h = 2 * (x // 2) + y, x % 2
 
         @pl.when(jnp.logical_not((k * owners + o == r) & (h == k)))
         def _():
@@ -352,6 +405,16 @@
     else:
         pl.when(r % stride == 0)(shared)
     pl.loop(0, own)(lambda p: pass_on(p).wait_send())
+
+
+def copy_out(*refs):
+    n = len(refs) // 2
+    sems = refs[-1]
+    copies = [pltpu.make_async_copy(refs[i], refs[n + i], sems.at[i]) for i in range(n)]
+    for copy in copies:
+        copy.start()
+    for copy in copies:
+        copy.wait()
 
 
 def local(rows, alignment_left, alignment_right, weight, pairwise_bias, cotangent):
@@ -367,7 +430,7 @@
     right = jnp.transpose(alignment_right, (1, 2, 0)).reshape(wide, half_s)
     vmem, dma = pltpu.VMEM, pltpu.SemaphoreType.DMA
     lanes = d2n * 128
-    pair, gl, gr, gw, gb = pl.pallas_call(
+    results = pl.pallas_call(
         functools.partial(kernel, rows, own),
         out_shape=(
             jax.ShapeDtypeStruct(cotangent.shape, BF16),
@@ -396,23 +459,33 @@
             vmem((2 * half_s, lanes), BF16),
             vmem((chan * d2n, ires * 128), BF16),
             vmem((owners, 2, half_s, wide), BF16),
-            vmem((rows, half_s, wide), BF16),
+            vmem((owners, half_s, wide), BF16),
             vmem((2, half_w, 2 * pair_dim), F32),
             vmem((half_w, 2 * pair_dim), F32),
             vmem((own, half_w // own, 2 * pair_dim), BF16),
             vmem((rows, half_w // own, 2 * pair_dim), BF16),
-            vmem((2, own, half_w // own, 2 * pair_dim), F32),
+            vmem((2, own, half_w // own, 2 * pair_dim), BF16),
             vmem((2, half_s, wide), F32),
             vmem((half_s, wide), F32),
             vmem((8, pair_dim), F32),
             vmem((2 * rows, 8, pair_dim), F32),
             dma((2,)), dma((rows,)), dma((owners, 2)), dma((owners, 2)), dma((rows,)),
             dma((2,)), dma((own,)), dma((rows,)), dma((rows,)), dma((2, own)), dma((own,)),
-            dma((2,)), dma((2 * rows,)), dma((2 * rows,)),
+            dma((2,)), dma((2 * rows,)), dma((2 * rows,)), dma((owners,)),
+            vmem((owners, half_s, wide), BF16),
+            dma((owners,)), dma((owners,)),
         ],
         compiler_params=pltpu.CompilerParams(
             collective_id=0, has_side_effects=True, vmem_limit_bytes=58 * 2**20),
     )(left, right, weight, pairwise_bias.reshape(1, pair_dim), cotangent)
+    pair, gl, gr, gw, gb = pl.pallas_call(
+        copy_out,
+        out_shape=tuple(jax.ShapeDtypeStruct(x.shape, x.dtype) for x in results),
+        in_specs=[pl.BlockSpec(memory_space=pl.ANY)] * 5,
+        out_specs=tuple([pl.BlockSpec(memory_space=pl.ANY)] * 5),
+        scratch_shapes=[dma((5,))],
+        compiler_params=pltpu.CompilerParams(vmem_limit_bytes=63 * 2**20),
+    )(*results)
     gl, gr = (jnp.transpose(x.reshape(chan, ires, half_s), (2, 0, 1)) for x in (gl, gr))
     return pair, gl, gr, gw, gb.reshape(pair_dim)
 

time: 50.6 us -> 84.5 us (1.67)
  Pallas kernels: 45 us -> 83.7 us
  local copies, waits for them, and re-layouts: 4.45 us -> 0 us
    pallas_call x0 -> x1, Pallas kernels: none -> 40.9 us  [local(): pl.pallas_call(copy_out, out_shape=tuple((jax.ShapeDtypeStruct(x.shape, x...]
    unnamed x13 -> x0, local copies, waits for them, and re-layouts: 4.45 us -> none
    pallas_call x1, Pallas kernels: 45 us -> 42.9 us  [local(): pl.pallas_call(functools.partial(kernel, rows, own), out_shape=(jax.Shape...]
where the time goes in v3:
time: 84.5 us; the launch traced here: 84.4 us
  Pallas kernels  83.7 us (99%)
    pallas_call x1, Pallas kernels, local(): pl.pallas_call(functools.partial(kernel, rows, own), out_shape=(jax.Shape...  42.9 us
    pallas_call x1, Pallas kernels, local(): pl.pallas_call(copy_out, out_shape=tuple((jax.ShapeDtypeStruct(x.shape, x...  40.9 us

profile of v3, /device:TPU:0, one launch (start us, length us, event | category | flops | bytes accessed | tf_op | source)
XLA Modules:
  0.0 84.4 jit_solution(10651878328038591304)
XLA Ops:
  0.6 42.9 %shard_map.92 = (bf16[16,64,128]{2,1,0:T(8,128)(2,1)}, f32[512,64]{1,0:T(8,128)}, f32[512,64]{1,0:T(8,128)}, f32[1024,128]{1,0:T(8,128)}, f32[1,128]{1,0:T(1,128)}) custom-call(bf16[512,64]{1,0:T(8,128)(2,1)} %bitcast.14, bf16[512,64]{1,0:T(8,128)(2,1)} %bitcast.15, bf16[1024,128]{1,0:T(8,128)(2,1)} %w_ref.1, bf16[1,128]{1,0:T(2,128)(2,1)} %bitcast.16, ...), custom_call_target="tpu_custom_call" | custom-call | tf_op jit(solution)/shard_map/pallas_call | solution.py:433
  43.5 40.9 %shard_map.93 = (bf16[16,64,128]{2,1,0:T(8,128)(2,1)}, f32[512,64]{1,0:T(8,128)}, f32[512,64]{1,0:T(8,128)}, f32[1024,128]{1,0:T(8,128)}, f32[1,128]{1,0:T(1,128)}) custom-call(bf16[16,64,128]{2,1,0:T(8,128)(2,1)} %get-tuple-element.15.refs_0_, f32[512,64]{1,0:T(8,128)} %get-tuple-element.16.refs_1_, f32[512,64]{1,0:T(8,128)} %get-tuple-element.17.refs_2_, ...), custom_call_target="tpu_custom_call" | custom-call | tf_op jit(solution)/shard_map/pallas_call | solution.py:481

commit v4 on v3

--- a/solution.py
+++ b/solution.py
@@ -56,49 +56,50 @@
         pl.semaphore_signal(barrier, inc=1, device_id=(g, q // 2, q % 2), device_id_type=MESH)
 
     rsend[...] = right_ref[...].astype(F32).T.astype(BF16)
-    pl.semaphore_wait(barrier, 2 * rows - 1)
-
-    def right_copy(t):
-        return remote(rsend, rbuf.at[ol, k], rssem.at[t], rsem.at[ol, k], (r + 2 * t) % rows, kt)
-
-    @pl.when(kt == k)
-    def _():
-        pltpu.make_async_copy(rsend, rbuf.at[ol, k], rsem.at[ol, k]).start()
-
-    @pl.when(kt != k)
-    def _():
-        remote(rsend, rbuf.at[ol, k], rssem.at[0], rsem.at[ol, k], r, sib).start()
-
-    peer_copy = remote(rsend, rbuf.at[ol, k], rssem.at[cols], rsem.at[ol, k], peer, kt)
-    peer_copy.start()
-
-    @pl.loop(1, cols)
-    def _(t):
-        right_copy(t).start()
-
-    def hand_on(x):
-        o, h = 2 * (x // 2) + y, x % 2
-        return remote(rbuf.at[o, h], rbuf.at[o, h], hsem.at[x], rsem.at[o, h], peer, k)
-
-    def not_mine(x):
-        return k * owners + 2 * (x // 2) + y != r
-
-    def hand_all():
-        @pl.loop(0, owners)
-        def _(x):
-            o, h = 2 * (x // 2) + y, x % 2
-            landed(rbuf.at[o, h], rsem.at[o, h])
-
-            @pl.when(not_mine(x))
-            def _():
-                hand_on(x).start()
-
     ibits, dbits = ires.bit_length() - 1, (128 // ires).bit_length() - 1
     pm = lax.broadcasted_iota(jnp.int32, (wide, wide), 0)
     pn = lax.broadcasted_iota(jnp.int32, (wide, wide), 1)
     goal = (pm & (ires - 1)) * chan + (pm >> ibits)
     perm2[...] = jnp.where(goal == pn, 1.0, 0.0).astype(BF16)
     lsend[...] = dot(left_ref[...], perm2[...], 0, 0).astype(BF16)
+    pl.semaphore_wait(barrier, 2 * rows - 1)
+
+    def right_copy(t):
+        return remote(rsend, rbuf.at[ol, k], rssem.at[t], rsem.at[ol, k], (r + 2 * t) % rows, kt)
+
+    @pl.when(kt == k)
+    def _():
+        pltpu.make_async_copy(rsend, rbuf.at[ol, k], rsem.at[ol, k]).start()
+
+    @pl.when(kt != k)
+    def _():
+        remote(rsend, rbuf.at[ol, k], rssem.at[0], rsem.at[ol, k], r, sib).start()
+
+    peer_copy = remote(rsend, rbuf.at[ol, k], rssem.at[cols], rsem.at[ol, k], peer, kt)
+
+    @pl.loop(1, cols)
+    def _(t):
+        right_copy(t).start()
+
+    peer_copy.start()
+
+    def hand_on(x):
+        o, h = 2 * (x // 2) + y, x % 2
+        return remote(rbuf.at[o, h], rbuf.at[o, h], hsem.at[x], rsem.at[o, h], peer, k)
+
+    def not_mine(x):
+        return k * owners + 2 * (x // 2) + y != r
+
+    def hand_all():
+        @pl.loop(0, owners)
+        def _(x):
+            o, h = 2 * (x // 2) + y, x % 2
+            landed(rbuf.at[o, h], rsem.at[o, h])
+
+            @pl.when(not_mine(x))
+            def _():
+                hand_on(x).start()
+
     left_copy = remote(lsend, lbuf.at[k], lsem.at[0], lsem.at[1], r, sib)
     left_copy.start()
 
@@ -142,8 +143,7 @@
     def grads(b):
         fill_bd(b)
 
-        @pl.loop(0, ires // 2)
-        def _(p):
+        def step(p):
             res = dot(w2[...], bd[pl.ds(pl.multiple_of(p * 256, 256), 256), :], 1, 1)
             for u in range(2):
                 scr[u] = res[:, u * 128 : u * 128 + 128]
@@ -153,8 +153,14 @@
                     grs[b, pl.ds(at, chan), q * 128 : q * 128 + 128] = scr[
                         u, pl.ds(q, chan, stride=d2n), :].astype(BF16)
 
+        pl.loop(0, ires // 4)(step)
+        if blocks == 1:
+            hand_all()
+        pl.loop(ires // 4, ires // 2)(step)
+
     each_block(grads)
-    hand_all()
+    if blocks > 1:
+        hand_all()
 
     left_copy.wait_recv()
     lm = lbuf[...].reshape(seqs, wide)
@@ -214,9 +220,6 @@
                  for o in range(per)], axis=1)
             rs[:, q * 512 : q * 512 + 512] = dot(cat, perm[...]).astype(BF16)
 
-        if blocks == 1:
-            pl.loop(0, owners)(right_sums)
-
         @pl.loop(0, d2n // 2)
         def _(p):
             res = dot(lt[...], rs[:, pl.ds(pl.multiple_of(p * 256, 256), 256)]) * inv_seqs
@@ -232,6 +235,8 @@
         if blocks == 1:
             weight_copy.start()
         weight_half(k)
+        if blocks == 1:
+            pl.loop(0, owners)(right_sums)
 
         @pl.loop(0, ires // 2)
         def _(p):
@@ -409,12 +414,8 @@
 
 def copy_out(*refs):
     n = len(refs) // 2
-    sems = refs[-1]
-    copies = [pltpu.make_async_copy(refs[i], refs[n + i], sems.at[i]) for i in range(n)]
-    for copy in copies:
-        copy.start()
-    for copy in copies:
-        copy.wait()
+    for i in range(n):
+        refs[n + i][...] = refs[i][...]
 
 
 def local(rows, alignment_left, alignment_right, weight, pairwise_bias, cotangent):
@@ -481,10 +482,9 @@
     pair, gl, gr, gw, gb = pl.pallas_call(
         copy_out,
         out_shape=tuple(jax.ShapeDtypeStruct(x.shape, x.dtype) for x in results),
-        in_specs=[pl.BlockSpec(memory_space=pl.ANY)] * 5,
-        out_specs=tuple([pl.BlockSpec(memory_space=pl.ANY)] * 5),
-        scratch_shapes=[dma((5,))],
-        compiler_params=pltpu.CompilerParams(vmem_limit_bytes=63 * 2**20),
+        in_specs=[pl.BlockSpec(memory_space=vmem)] * 5,
+        out_specs=tuple([pl.BlockSpec(memory_space=vmem)] * 5),
+        compiler_params=pltpu.CompilerParams(vmem_limit_bytes=58 * 2**20),
     )(*results)
     gl, gr = (jnp.transpose(x.reshape(chan, ires, half_s), (2, 0, 1)) for x in (gl, gr))
     return pair, gl, gr, gw, gb.reshape(pair_dim)

time: 84.5 us -> 46.3 us (0.55)
  Pallas kernels: 83.7 us -> 45.3 us
    pallas_call x1, Pallas kernels: 40.9 us -> 2.34 us  [local(): pl.pallas_call(copy_out, out_shape=tuple((jax.ShapeDtypeStruct(x.shape, x...]
where the time goes in v4:
time: 46.3 us; the launch traced here: 45.9 us
  Pallas kernels  45.3 us (98%)
  between operations  0.64 us (1%)
    pallas_call x1, Pallas kernels, local(): pl.pallas_call(functools.partial(kernel, rows, own), out_shape=(jax.Shape...  42.9 us
    pallas_call x1, Pallas kernels, local(): pl.pallas_call(copy_out, out_shape=tuple((jax.ShapeDtypeStruct(x.shape, x...  2.34 us

profile of v4, /device:TPU:0, one launch (start us, length us, event | category | flops | bytes accessed | tf_op | source)
XLA Modules:
  0.0 45.9 jit_solution(5967980146082521303)
XLA Ops:
  0.6 42.9 %shard_map.92 = (bf16[16,64,128]{2,1,0:T(8,128)(2,1)}, f32[512,64]{1,0:T(8,128)}, f32[512,64]{1,0:T(8,128)}, f32[1024,128]{1,0:T(8,128)}, f32[1,128]{1,0:T(1,128)}) custom-call(bf16[512,64]{1,0:T(8,128)(2,1)} %bitcast.14, bf16[512,64]{1,0:T(8,128)(2,1)} %bitcast.15, bf16[1024,128]{1,0:T(8,128)(2,1)} %w_ref.1, bf16[1,128]{1,0:T(2,128)(2,1)} %bitcast.16, ...), custom_call_target="tpu_custom_call" | custom-call | tf_op jit(solution)/shard_map/pallas_call | solution.py:434
  43.6 2.3 %shard_map.93 = (bf16[16,64,128]{2,1,0:T(8,128)(2,1)}, f32[512,64]{1,0:T(8,128)}, f32[512,64]{1,0:T(8,128)}, f32[1024,128]{1,0:T(8,128)}, f32[1,128]{1,0:T(1,128)}) custom-call(bf16[16,64,128]{2,1,0:T(8,128)(2,1)} %get-tuple-element.15.refs_0_, f32[512,64]{1,0:T(8,128)} %get-tuple-element.16.refs_1_, f32[512,64]{1,0:T(8,128)} %get-tuple-element.17.refs_2_, ...), custom_call_target="tpu_custom_call" | custom-call | tf_op jit(solution)/shard_map/pallas_call | solution.py:482

commit v5 on v4

--- a/solution.py
+++ b/solution.py
@@ -296,6 +296,54 @@
         def _():
             weight_send(p).start()
 
+    inv_rows = 1.0 / (ires * rows)
+    me = r // stride
+
+    def share(t):
+        return remote(agbuf.at[k, me], agbuf.at[k, me], assem.at[t], asem.at[k, me], (r + t) % rows, k)
+
+    def pass_on(p):
+        return remote(agbuf.at[k, p], agbuf.at[k, p], fsem.at[p], asem.at[k, p], r, sib)
+
+    def own_slice():
+        def add(q, acc):
+            landed(wr.at[q], wrsem.at[q])
+            return acc + wr[q].astype(F32)
+
+        mean = lax.fori_loop(0, rows, add, jnp.zeros((slab, 256), F32)) * inv_rows
+        agbuf[k, me] = mean.astype(BF16)
+        pl.loop(1, rows)(lambda t: share(t).start())
+        pass_on(me).start()
+
+    if stride == 1:
+        own_slice()
+    else:
+        pl.when(r % stride == 0)(own_slice)
+
+    gl_copy.wait_recv()
+    gls[...] = ((glacc[k] + glsib[...]) * inv_seqs).T
+    for i in range(ires):
+        gl_ref[pl.ds(i, chan, stride=ires), :] = gls[i * chan : (i + 1) * chan, :]
+
+    def add_bias(q, acc):
+        @pl.when(q != 2 * r + k)
+        def _():
+            landed(bbuf.at[q], bsem.at[q])
+
+        return acc + bbuf[q]
+
+    bias_sum = lax.fori_loop(0, 2 * rows, add_bias, jnp.zeros(bsend.shape, F32)) * inv_rows
+    gb_ref[...] = bias_sum[0:1, :]
+
+    @pl.loop(0, own)
+    def _(t):
+        p = (me + t) % own
+
+        @pl.when(p * stride != r)
+        def _():
+            landed(agbuf.at[k, p], asem.at[k, p])
+            pass_on(p).start()
+
     total = jnp.zeros((half_s, wide), F32)
     if rows <= 8:
         for q in range(cols):
@@ -309,54 +357,6 @@
         def _(q):
             landed(gbuf.at[q], gsem.at[q])
             gr_ref[...] += (gbuf[q].astype(F32) * inv_seqs).T
-
-    inv_rows = 1.0 / (ires * rows)
-    me = r // stride
-
-    def share(t):
-        return remote(agbuf.at[k, me], agbuf.at[k, me], assem.at[t], asem.at[k, me], (r + t) % rows, k)
-
-    def pass_on(p):
-        return remote(agbuf.at[k, p], agbuf.at[k, p], fsem.at[p], asem.at[k, p], r, sib)
-
-    def own_slice():
-        def add(q, acc):
-            landed(wr.at[q], wrsem.at[q])
-            return acc + wr[q].astype(F32)
-
-        mean = lax.fori_loop(0, rows, add, jnp.zeros((slab, 256), F32)) * inv_rows
-        agbuf[k, me] = mean.astype(BF16)
-        pl.loop(1, rows)(lambda t: share(t).start())
-        pass_on(me).start()
-
-    if stride == 1:
-        own_slice()
-    else:
-        pl.when(r % stride == 0)(own_slice)
-
-    gl_copy.wait_recv()
-    gls[...] = ((glacc[k] + glsib[...]) * inv_seqs).T
-    for i in range(ires):
-        gl_ref[pl.ds(i, chan, stride=ires), :] = gls[i * chan : (i + 1) * chan, :]
-
-    def add_bias(q, acc):
-        @pl.when(q != 2 * r + k)
-        def _():
-            landed(bbuf.at[q], bsem.at[q])
-
-        return acc + bbuf[q]
-
-    bias_sum = lax.fori_loop(0, 2 * rows, add_bias, jnp.zeros(bsend.shape, F32)) * inv_rows
-    gb_ref[...] = bias_sum[0:1, :]
-
-    @pl.loop(0, own)
-    def _(t):
-        p = (me + t) % own
-
-        @pl.when(p * stride != r)
-        def _():
-            landed(agbuf.at[k, p], asem.at[k, p])
-            pass_on(p).start()
 
     @pl.loop(0, own)
     def _(p):

time: 46.3 us -> 45.9 us (level)
  no operation moved by 1% of the time
where the time goes in v5:
time: 45.9 us; the launch traced here: 45.7 us
  Pallas kernels  45.1 us (98%)
  between operations  0.64 us (1%)
    pallas_call x1, Pallas kernels, local(): pl.pallas_call(functools.partial(kernel, rows, own), out_shape=(jax.Shape...  42.7 us
    pallas_call x1, Pallas kernels, local(): pl.pallas_call(copy_out, out_shape=tuple((jax.ShapeDtypeStruct(x.shape, x...  2.34 us

profile of v5, /device:TPU:0, one launch (start us, length us, event | category | flops | bytes accessed | tf_op | source)
XLA Modules:
  0.0 45.7 jit_solution(12266369470289010054)
XLA Ops:
  0.6 42.7 %shard_map.92 = (bf16[16,64,128]{2,1,0:T(8,128)(2,1)}, f32[512,64]{1,0:T(8,128)}, f32[512,64]{1,0:T(8,128)}, f32[1024,128]{1,0:T(8,128)}, f32[1,128]{1,0:T(1,128)}) custom-call(bf16[512,64]{1,0:T(8,128)(2,1)} %bitcast.14, bf16[512,64]{1,0:T(8,128)(2,1)} %bitcast.15, bf16[1024,128]{1,0:T(8,128)(2,1)} %w_ref.1, bf16[1,128]{1,0:T(2,128)(2,1)} %bitcast.16, ...), custom_call_target="tpu_custom_call" | custom-call | tf_op jit(solution)/shard_map/pallas_call | solution.py:434
  43.4 2.3 %shard_map.93 = (bf16[16,64,128]{2,1,0:T(8,128)(2,1)}, f32[512,64]{1,0:T(8,128)}, f32[512,64]{1,0:T(8,128)}, f32[1024,128]{1,0:T(8,128)}, f32[1,128]{1,0:T(1,128)}) custom-call(bf16[16,64,128]{2,1,0:T(8,128)(2,1)} %get-tuple-element.15.refs_0_, f32[512,64]{1,0:T(8,128)} %get-tuple-element.16.refs_1_, f32[512,64]{1,0:T(8,128)} %get-tuple-element.17.refs_2_, ...), custom_call_target="tpu_custom_call" | custom-call | tf_op jit(solution)/shard_map/pallas_call | solution.py:482
